TPU v7x, 32 devices: a whole 2x2x4 slice. The times are simulated.
32 devices in a mesh: wide: 16 (over z, x, core), narrow: 2 (over y).
Axes of the slice: x: 2, y: 2, z: 4, core: 2. Of those that a mesh axis runs over, the one named last changes fastest.
Arguments:
- charges: float32 [64, 65536], P(None, ('wide', 'narrow')), may hold values from -6 to 6
- leaf_angle: float32 [64, 4096], P(None, ('wide', 'narrow')), may hold values from -3.140625 to 3.140625
- lagrange: float32 [48, 64], replicated, may hold values from -0.75 to 0.75
- level_angle: float32 [2, 48, 4096], P(None, None, ('wide', 'narrow')), may hold values from -3.140625 to 3.140625
- level_self: float32 [2, 96, 96], replicated, may hold values from -0.4375 to 0.4375
- level_peer: float32 [2, 96, 96], replicated, may hold values from -0.4375 to 0.4375
- switch_angle: float32 [48, 4096], P(None, ('wide', 'narrow')), may hold values from -3.140625 to 3.140625
- switch_matrix: float32 [96, 96], replicated, may hold values from -0.625 to 0.625
- out_angle: float32 [64, 4096], P(None, ('wide', 'narrow')), may hold values from -3.140625 to 3.140625
- evaluate: float32 [64, 48], replicated, may hold values from -0.875 to 0.875
Outputs:
- field: bfloat16 [64, 65536], P(None, ('wide', 'narrow'))
All inputs are finite; a program needn't handle non-finite values.
Results may differ from a plain program's by a relative error of at most 0.0049.
Values may be sent and summed in bfloat16 or wider, within the bound.
A program may use at most 64 MiB of HBM per device.

v0:
```python
import jax
import jax.numpy as jnp
from jax import lax
from jax.sharding import PartitionSpec as P


def from_partner(value, axis, apart):
    mask = 2**apart
    pairs = [(source, source ^ mask) for source in range(lax.axis_size(axis))]
    return lax.ppermute(value, axis, pairs)


def product(left, right):
    return jnp.dot(left, right, precision=lax.Precision.HIGHEST, preferred_element_type=jnp.float32)


def rotate(boxes_state, phase_angle, per_box):
    rank = phase_angle.shape[0]
    cos_part = jnp.repeat(jnp.cos(phase_angle), per_box, axis=1)
    sin_part = jnp.repeat(jnp.sin(phase_angle), per_box, axis=1)
    real_part = boxes_state[:rank]
    imag_part = boxes_state[rank:]
    return jnp.concatenate(
        [cos_part * real_part - sin_part * imag_part, sin_part * real_part + cos_part * imag_part],
        axis=0,
    )


def butterfly_level(boxes_state, self_matrix, peer_matrix, phase_angle, bit, per_box):
    sent_state = boxes_state.astype(jnp.bfloat16)
    received = from_partner(sent_state, "narrow", bit)
    combined = product(self_matrix, boxes_state) + product(
        peer_matrix, received.astype(jnp.float32)
    )
    return rotate(combined, phase_angle, per_box)


def leaf_weights(lagrange, point_charges, point_angle, per_box):
    cos_leaf = jnp.repeat(jnp.cos(point_angle), per_box, axis=1)
    sin_leaf = jnp.repeat(jnp.sin(point_angle), per_box, axis=1)
    return jnp.concatenate(
        [product(lagrange, cos_leaf * point_charges), product(lagrange, sin_leaf * point_charges)],
        axis=0,
    )


def body(
    charges,
    leaf_angle,
    lagrange,
    level_angle,
    level_self,
    level_peer,
    switch_angle,
    switch_matrix,
    out_angle,
    evaluate,
):
    per_box = charges.shape[1] // leaf_angle.shape[1]
    rank = lagrange.shape[0]
    last_bit = lax.axis_size("narrow").bit_length() - 2
    boxes_state = leaf_weights(lagrange, charges, leaf_angle, per_box)
    boxes_state = butterfly_level(
        boxes_state, level_self[0], level_peer[0], level_angle[0], 0, per_box
    )
    boxes_state = lax.all_to_all(boxes_state, "wide", split_axis=1, concat_axis=1, tiled=True)
    boxes_state = rotate(product(switch_matrix, boxes_state), switch_angle, per_box)
    boxes_state = butterfly_level(
        boxes_state, level_self[1], level_peer[1], level_angle[1], last_bit, per_box
    )
    real_part = product(evaluate, boxes_state[:rank])
    imag_part = product(evaluate, boxes_state[rank:])
    cos_out = jnp.repeat(jnp.cos(out_angle), per_box, axis=1)
    sin_out = jnp.repeat(jnp.sin(out_angle), per_box, axis=1)
    return (cos_out * real_part - sin_out * imag_part).astype(jnp.bfloat16)


def solution(mesh):
    return jax.shard_map(
        body,
        mesh=mesh,
        in_specs=(
            P(None, ("wide", "narrow")),
            P(None, ("wide", "narrow")),
            P(),
            P(None, None, ("wide", "narrow")),
            P(),
            P(),
            P(None, ("wide", "narrow")),
            P(),
            P(None, ("wide", "narrow")),
            P(),
        ),
        out_specs=P(None, ("wide", "narrow")),
        check_vma=False,
    )
```

profile of v0, /device:TPU:0, one launch (start us, length us, event | category | flops | bytes accessed | tf_op | source)
XLA Modules:
  0.0 61.7 jit_solution(10447675349360832506)
XLA Ops:
  0.0 0.9 %fusion.33 = (f32[64,128]{1,0:T(8,128)S(1)}, f32[64,128]{1,0:T(8,128)S(1)}) fusion(f32[64,128]{1,0:T(8,128)} %param.11), kind=kLoop, calls=%fused_computation.54 | loop fusion | bytes 98304 | tf_op jit(solution)/shard_map/cos | solution.py:39
  0.9 0.1 copy.68
  1.0 0.1 copy.70
  1.1 1.4 %copy.69 = f32[64,2048]{0,1:T(8,128)S(1)} copy(f32[64,2048]{1,0:T(8,128)} %param.10) | data formatting | bytes 1048576 | tf_op args[0]
  2.5 0.0 copy-start.8
  2.5 0.1 bitcast_multiply_fusion.1
  2.6 0.6 copy-done.8
  3.2 1.3 %convolution_bitcast_fusion.3 = f32[48,2048]{1,0:T(8,128)S(1)} fusion(f32[64,2048]{0,1:T(8,128)S(1)} %get-tuple-element.10, f32[48,64]{1,0:T(8,128)S(1)} %copy-done.8), kind=kOutput, calls=%fused_computation.11 | convolution fusion | flops 75497472 | bytes 929792 | tf_op jit(solution)/shard_map/dot_general | solution.py:14
  4.5 1.3 %convolution_bitcast_fusion.4 = f32[48,2048]{1,0:T(8,128)S(1)} fusion(f32[64,2048]{0,1:T(8,128)S(1)} %get-tuple-element.9, f32[48,64]{1,0:T(8,128)S(1)} %copy-done.8), kind=kOutput, calls=%fused_computation.12 | convolution fusion | flops 75497472 | bytes 929792 | tf_op jit(solution)/shard_map/dot_general | solution.py:14
  5.8 0.0 copy-start.9
  5.8 3.0 %collective-permute-start = (bf16[96,2048]{1,0:T(8,128)(2,1)S(1)}, bf16[96,2048]{1,0:T(8,128)(2,1)S(1)}, u32[]{:S(2)}, u32[]{:S(2)}) collective-permute-start(bf16[96,2048]{1,0:T(8,128)(2,1)S(1)} %fusion.10), channel_id=1, source_target_pairs={{0,1},{1,0},{2,3},{3,2},{4,5},{5,4},{6,7},{7,6},{8,9},{9,8},{10,11... | collective-permute-start | bytes 1179656 | tf_op jit(solution)/shard_map/ppermute | solution.py:10
  8.9 0.8 %sine_bitcast_fusion.1 = (f32[48,128]{1,0:T(8,128)S(1)}, f32[48,128]{1,0:T(8,128)}, f32[48,128]{1,0:T(8,128)S(1)}, f32[48,128]{1,0:T(8,128)}) fusion(f32[2,48,128]{2,1,0:T(8,128)S(1)} %copy-done.9), kind=kLoop, calls=%fused_computation.48 | loop fusion | bytes 147456 | tf_op jit(solution)/shard_map/sin | solution.py:20
  9.7 0.1 copy.67
  9.8 0.1 broadcast_in_dim.33
  9.8 0.3 copy.72
  10.1 0.1 copy.73
  10.2 0.1 broadcast_in_dim.36
  10.3 0.0 copy-start.3
  10.3 0.3 copy.74
  10.6 0.6 copy-done.3
  11.2 0.8 %fusion.11 = f32[2048,96]{0,1:T(8,128)S(1)} fusion(f32[48,2048]{1,0:T(8,128)S(1)} %convolution_bitcast_fusion.3, f32[48,2048]{1,0:T(8,128)S(1)} %convolution_bitcast_fusion.4, f32[2,96,96]{2,1,0:T(8,128)S(1)} %copy-done.3), kind=kOutput, calls=%fused_computation.24 | convolution fusion | flops 226689024 | bytes 1622016 | tf_op jit(solution)/shard_map/dot_general | solution.py:14
  12.1 5.9 %collective-permute-done = bf16[96,2048]{1,0:T(8,128)(2,1)S(1)} collective-permute-done((bf16[96,2048]{1,0:T(8,128)(2,1)S(1)}, bf16[96,2048]{1,0:T(8,128)(2,1)S(1)}, u32[]{:S(2)}, u32[]{:S(2)}) %collective-permute-start) | collective-permute-done | bytes 393248 | tf_op jit(solution)/shard_map/ppermute | solution.py:10
  18.0 0.0 copy-done.6
  18.0 0.5 fusion.1
  18.4 0.1 multiply_subtract_fusion.1
  18.5 1.0 %copy_bitcast_fusion = f32[96,16,128]{2,0,1:T(8,128)} fusion(f32[48,2048]{1,0:T(8,128)S(1)} %get-tuple-element.8, f32[48,2048]{1,0:T(8,128)S(1)} %get-tuple-element.7), kind=kLoop, calls=%fused_computation.17 | loop fusion | flops 196608 | bytes 1572864 | tf_op jit(solution)/shard_map/all_to_all | solution.py:66
  19.5 6.3 %all-to-all-start = ((f32[96,16,128]{2,0,1:T(8,128)}), f32[96,16,128]{2,0,1:T(8,128)S(1)}, u32[]{:S(2)}, u32[]{:S(2)}) async-start(f32[96,16,128]{2,0,1:T(8,128)} %copy_bitcast_fusion), calls=%async_computation | async-start | bytes 1572864 | tf_op jit(solution)/shard_map/all_to_all | solution.py:66
  25.8 0.1 fusion.34
  25.9 0.1 copy.66
  26.0 0.1 broadcast_in_dim.32
  26.1 0.3 copy.79
  26.4 0.1 copy.80
  26.5 0.1 broadcast_in_dim.37
  26.6 0.3 copy.81
  26.9 0.4 copy-done.5
  27.3 0.1 copy.65
  27.4 0.1 broadcast_in_dim.31
  27.5 0.0 copy-start.4
  27.5 0.3 copy.84
  27.8 0.4 copy-done.4
  28.2 0.1 copy.85
  28.3 0.1 broadcast_in_dim.38
  28.4 0.3 copy.86
  28.7 15.8 %all-to-all-done = f32[96,16,128]{2,0,1:T(8,128)S(1)} async-done(((f32[96,16,128]{2,0,1:T(8,128)}), f32[96,16,128]{2,0,1:T(8,128)S(1)}, u32[]{:S(2)}, u32[]{:S(2)}) %all-to-all-start) | async-done | bytes 786464 | tf_op jit(solution)/shard_map/all_to_all | solution.py:66
  44.5 0.8 %convolution_bitcast_fusion = f32[96,2048]{1,0:T(8,128)S(1)} fusion(f32[96,96]{1,0:T(8,128)S(1)} %copy-done, f32[96,16,128]{2,0,1:T(8,128)S(1)} %all-to-all-done), kind=kOutput, calls=%fused_computation | convolution fusion | flops 226492416 | bytes 1609728 | tf_op jit(solution)/shard_map/dot_general | solution.py:14
  45.4 0.1 multiply_subtract_fusion
  45.5 0.0 copy-start.10
  45.5 0.8 %fusion.8 = bf16[96,2048]{1,0:T(8,128)(2,1)} fusion(f32[48,2048]{1,0:T(8,128)S(1)} %get-tuple-element.6, f32[48,2048]{1,0:T(8,128)S(1)} %get-tuple-element.5), kind=kLoop, calls=%fused_computation.21 | loop fusion | flops 786432 | bytes 1179648 | tf_op jit(solution)/shard_map/convert_element_type | solution.py:30
  46.3 1.5 %collective-permute-start.1 = (bf16[96,2048]{1,0:T(8,128)(2,1)}, bf16[96,2048]{1,0:T(8,128)(2,1)}, u32[]{:S(2)}, u32[]{:S(2)}) collective-permute-start(bf16[96,2048]{1,0:T(8,128)(2,1)} %fusion.8), channel_id=1, source_target_pairs={{0,1},{1,0},{2,3},{3,2},{4,5},{5,4},{6,7},{7,6},{8,9},{9,8},{10,11... | collective-permute-start | bytes 1179656 | tf_op jit(solution)/shard_map/ppermute | solution.py:10
  47.8 0.0 copy-done.10
  47.8 0.1 fusion.32
  47.9 0.1 copy.64
  48.0 0.1 broadcast_in_dim.30
  48.1 0.3 copy.87
  48.4 0.1 copy.88
  48.5 0.1 broadcast_in_dim.39
  48.6 1.1 %copy.91 = f32[64,2048]{1,0:T(8,128)} copy(f32[64,2048]{0,1:T(8,128)S(1)} %bitcast.82) | data formatting | bytes 1048576 | tf_op jit(solution)/shard_map/reshape | solution.py:74
  49.7 0.8 %fusion.9 = f32[2048,96]{0,1:T(8,128)S(1)} fusion(f32[48,2048]{1,0:T(8,128)S(1)} %get-tuple-element.6, f32[48,2048]{1,0:T(8,128)S(1)} %get-tuple-element.5, f32[2,96,96]{2,1,0:T(8,128)S(1)} %copy-done.3), kind=kOutput, calls=%fused_computation.22 | convolution fusion | flops 226689024 | bytes 1622016 | tf_op jit(solution)/shard_map/dot_general | solution.py:14
  50.6 0.0 copy-start.2
  50.6 7.3 %collective-permute-done.1 = bf16[96,2048]{1,0:T(8,128)(2,1)} collective-permute-done((bf16[96,2048]{1,0:T(8,128)(2,1)}, bf16[96,2048]{1,0:T(8,128)(2,1)}, u32[]{:S(2)}, u32[]{:S(2)}) %collective-permute-start.1) | collective-permute-done | bytes 393248 | tf_op jit(solution)/shard_map/ppermute | solution.py:10
  57.9 1.5 %fusion = f32[96,2048]{1,0:T(8,128)S(1)} fusion(f32[2048,96]{0,1:T(8,128)S(1)} %fusion.9, bf16[96,2048]{1,0:T(8,128)(2,1)} %collective-permute-done.1, f32[2,96,96]{2,1,0:T(8,128)S(1)} %copy-done.7), kind=kOutput, calls=%fused_computation.2 | convolution fusion | flops 226689024 | bytes 2015232 | tf_op jit(solution)/shard_map/dot_general | solution.py:14
  59.4 0.6 %fusion.4 = f32[64,2048]{1,0:T(8,128)S(1)} fusion(f32[64,2048]{1,0:T(8,128)S(1)} %copy.87, f32[64,48]{0,1:T(8,128)S(1)} %copy-done.2, f32[48,2048]{1,0:T(8,128)S(1)} %copy.86, f32[48,2048]{1,0:T(8,128)S(1)} %copy.84, f32[96,2048]{1,0:T(8,128)S(1)} %fusion), kind=kOutput, calls=%fused_computation.9 | convolution fusion | flops 75923456 | bytes 2633728 | tf_op jit(solution)/shard_map/dot_general | solution.py:14
  60.0 0.4 copy-done.1
  60.4 1.3 %fusion.5 = bf16[64,2048]{1,0:T(8,128)(2,1)} fusion(f32[64,2048]{1,0:T(8,128)S(1)} %fusion.4, f32[64,2048]{1,0:T(8,128)S(1)} %copy-done.1, f32[64,48]{0,1:T(8,128)S(1)} %copy-done.2, f32[48,2048]{1,0:T(8,128)S(1)} %copy.84, f32[48,2048]{1,0:T(8,128)S(1)} %copy.86, f32[96,2048]{1,0:T(8,128)S(1)} %fusion), kind=kOutput, calls=%fused_computation.10 | convolution fusion | flops 76185600 | bytes 2895872 | tf_op jit(solution)/shard_map/dot_general | solution.py:14
  (12 shorter events, 0.1 us)
Async XLA Ops:
  0.0 44.5 %copy-start = (f32[96,96]{1,0:T(8,128)S(1)}, f32[96,96]{1,0:T(8,128)}, u32[]{:S(2)}) copy-start(f32[96,96]{1,0:T(8,128)} %param.17) | copy-start | bytes 110596
  2.5 0.7 %copy-start.8 = (f32[48,64]{1,0:T(8,128)S(1)}, f32[48,64]{1,0:T(8,128)}, u32[]{:S(2)}) copy-start(f32[48,64]{1,0:T(8,128)} %param.12) | copy-start | bytes 36868
  5.8 3.1 %copy-start.9 = (f32[2,48,128]{2,1,0:T(8,128)S(1)}, f32[2,48,128]{2,1,0:T(8,128)}, u32[]{:S(2)}) copy-start(f32[2,48,128]{2,1,0:T(8,128)} %param.13) | copy-start | bytes 147460
  5.8 12.1 %collective-permute-start = (bf16[96,2048]{1,0:T(8,128)(2,1)S(1)}, bf16[96,2048]{1,0:T(8,128)(2,1)S(1)}, u32[]{:S(2)}, u32[]{:S(2)}) collective-permute-start(bf16[96,2048]{1,0:T(8,128)(2,1)S(1)} %fusion.10), channel_id=1, source_target_pairs={{0,1},{1,0},{2,3},{3,2},{4,5},{5,4},{6,7},{7,6},{8,9},{9,8},{10,11... | collective-permute-start | bytes 1179656 | tf_op jit(solution)/shard_map/ppermute | solution.py:10
  10.3 0.9 %copy-start.3 = (f32[2,96,96]{2,1,0:T(8,128)S(1)}, f32[2,96,96]{2,1,0:T(8,128)}, u32[]{:S(2)}) copy-start(f32[2,96,96]{2,1,0:T(8,128)} %param.14) | copy-start | bytes 221188
  11.2 6.8 %copy-start.6 = (f32[2,96,96]{2,1,0:T(8,128)S(1)}, f32[2,96,96]{2,1,0:T(8,128)}, u32[]{:S(2)}) copy-start(f32[2,96,96]{2,1,0:T(8,128)} %param.15) | copy-start | bytes 221188
  19.5 6.3 %copy-start.11 = (f32[48,128]{1,0:T(8,128)S(1)}, f32[48,128]{1,0:T(8,128)}, u32[]{:S(2)}) copy-start(f32[48,128]{1,0:T(8,128)} %param.16) | copy-start | bytes 73732
  19.5 25.0 %all-to-all-start = ((f32[96,16,128]{2,0,1:T(8,128)}), f32[96,16,128]{2,0,1:T(8,128)S(1)}, u32[]{:S(2)}, u32[]{:S(2)}) async-start(f32[96,16,128]{2,0,1:T(8,128)} %copy_bitcast_fusion), calls=%async_computation | async-start | bytes 1572864 | tf_op jit(solution)/shard_map/all_to_all | solution.py:66
  26.6 0.7 %copy-start.5 = (f32[48,128]{1,0:T(8,128)S(1)}, f32[48,128]{1,0:T(8,128)}, u32[]{:S(2)}) copy-start(f32[48,128]{1,0:T(8,128)} %get-tuple-element.14) | copy-start | bytes 73732
  27.5 0.7 %copy-start.4 = (f32[48,128]{1,0:T(8,128)S(1)}, f32[48,128]{1,0:T(8,128)}, u32[]{:S(2)}) copy-start(f32[48,128]{1,0:T(8,128)} %get-tuple-element.12) | copy-start | bytes 73732
  45.5 2.3 %copy-start.10 = (f32[64,128]{1,0:T(8,128)S(1)}, f32[64,128]{1,0:T(8,128)}, u32[]{:S(2)}) copy-start(f32[64,128]{1,0:T(8,128)} %param.18) | copy-start | bytes 98308
  46.3 11.6 %collective-permute-start.1 = (bf16[96,2048]{1,0:T(8,128)(2,1)}, bf16[96,2048]{1,0:T(8,128)(2,1)}, u32[]{:S(2)}, u32[]{:S(2)}) collective-permute-start(bf16[96,2048]{1,0:T(8,128)(2,1)} %fusion.8), channel_id=1, source_target_pairs={{0,1},{1,0},{2,3},{3,2},{4,5},{5,4},{6,7},{7,6},{8,9},{9,8},{10,11... | collective-permute-start | bytes 1179656 | tf_op jit(solution)/shard_map/ppermute | solution.py:10
  49.7 8.1 %copy-start.7 = (f32[2,96,96]{2,1,0:T(8,128)S(1)}, f32[2,96,96]{2,1,0:T(8,128)}, u32[]{:S(2)}) copy-start(f32[2,96,96]{2,1,0:T(8,128)} %param.15) | copy-start | bytes 221188
  50.6 8.8 %copy-start.2 = (f32[64,48]{0,1:T(8,128)S(1)}, f32[64,48]{0,1:T(8,128)}, u32[]{:S(2)}) copy-start(f32[64,48]{0,1:T(8,128)} %param.19) | copy-start | bytes 36868
  59.3 1.0 %copy-start.1 = (f32[64,2048]{1,0:T(8,128)S(1)}, f32[64,2048]{1,0:T(8,128)}, u32[]{:S(2)}) copy-start(f32[64,2048]{1,0:T(8,128)} %copy.91) | copy-start | bytes 1572868
where the time goes:
time: 62.4 us; the launch traced here: 61.7 us
  waiting for transfers between devices  29 us (46%)
  starting transfers between devices  10.8 us (17%)
  local copies, waits for them, and re-layouts  10.5 us (17%)
  matrix products  8.91 us (14%)
  other arithmetic  2.16 us (3%)
    all_to_all x1, waiting for transfers between devices, body(): lax.all_to_all(boxes_state, 'wide', split_axis=1, concat_axis=1, tiled=True)  15.8 us
    ppermute x2, waiting for transfers between devices, from_partner(): return lax.ppermute(value, axis, pairs)  13.2 us
    dot_general x9, matrix products, product(): jnp.dot(left, right, precision=lax.Precision.HIGHEST, preferred_element_t...  8.91 us
    all_to_all x1, starting transfers between devices, body(): lax.all_to_all(boxes_state, 'wide', split_axis=1, concat_axis=1, tiled=True)  6.26 us
    ppermute x2, starting transfers between devices, from_partner(): return lax.ppermute(value, axis, pairs)  4.55 us
    unnamed x25, local copies, waits for them, and re-layouts  3.82 us
  transfers between devices with their start and end apart: 3, of which 3 were waited for; matrix products, arithmetic and copies ran while one was open for 12% of the time, Pallas kernels for 0%

commit v1 on v0

--- a/solution.py
+++ b/solution.py
@@ -1,7 +1,15 @@
+import functools
+
 import jax
 import jax.numpy as jnp
 from jax import lax
+from jax.experimental import pallas as pl
+from jax.experimental.pallas import tpu as pltpu
 from jax.sharding import PartitionSpec as P
+
+MESH = pl.DeviceIdType.MESH
+F32 = jnp.float32
+BF16 = jnp.bfloat16
 
 
 def from_partner(value, axis, apart):
@@ -44,7 +52,7 @@
     )
 
 
-def body(
+def staged_body(
     charges,
     leaf_angle,
     lagrange,
@@ -75,22 +83,340 @@
     return (cos_out * real_part - sin_out * imag_part).astype(jnp.bfloat16)
 
 
+def cos_sin(angle):
+    half = angle * 0.5
+    t = half * half
+    s = half * (
+        1.0
+        + t * (-1 / 6 + t * (1 / 120 + t * (-1 / 5040 + t * (1 / 362880 + t * (-1 / 39916800)))))
+    )
+    c = 1.0 + t * (
+        -1 / 2
+        + t * (1 / 24 + t * (-1 / 720 + t * (1 / 40320 + t * (-1 / 3628800 + t / 479001600))))
+    )
+    return 1.0 - 2.0 * s * s, 2.0 * s * c
+
+
+def split(value):
+    high = value.astype(BF16)
+    return high, (value - high.astype(F32)).astype(BF16)
+
+
+def dot(left, right):
+    return jnp.dot(left, right, preferred_element_type=F32)
+
+
+def spread(boxes, columns, first, per_box):
+    box = lax.broadcasted_iota(jnp.int32, (boxes, columns), 0)
+    column = lax.broadcasted_iota(jnp.int32, (boxes, columns), 1) + first * per_box
+    low = box * per_box
+    once = jnp.where((column >= low) & (column < low + per_box), 1.0, 0.0).astype(BF16)
+    return jnp.concatenate([once, once], axis=0)
+
+
+def flip(index, bits):
+    if bits == 0:
+        return index
+    if bits == 1:
+        return index + 1 - 2 * lax.rem(index, 2)
+    if bits == 2:
+        return lax.rem(index + 2, 4)
+    return 3 - index
+
+
+def turn(real, imag, cos_part, sin_part):
+    return cos_part * real - sin_part * imag, sin_part * real + cos_part * imag
+
+
+def kernel(
+    per_box,
+    charges,
+    leaf_angle,
+    lagrange,
+    level_angle,
+    level_self,
+    level_peer,
+    switch_angle,
+    switch_matrix,
+    out_angle,
+    evaluate,
+    field,
+    outbox,
+    own,
+    peer,
+    peer_switch,
+    cos_table,
+    sin_table,
+    cos_peer,
+    sin_peer,
+    wide_send,
+    wide_recv,
+    narrow_send,
+    narrow_recv,
+    switch_sems,
+):
+    me = lax.axis_index("wide")
+    row = lax.axis_index("narrow")
+    layer = me // 4
+    place = lax.rem(me, 4)
+    other = 1 - row
+    rank, points = lagrange.shape
+    angles = points + rank
+
+    barrier = pltpu.get_barrier_semaphore()
+    for bits in range(1, 16):
+        to = flip(layer, bits // 4) * 4 + flip(place, bits % 4)
+        pl.semaphore_signal(barrier, inc=1, device_id={"wide": to}, device_id_type=MESH)
+    pl.semaphore_signal(barrier, inc=1, device_id={"narrow": other}, device_id_type=MESH)
+
+    stacked = jnp.concatenate(
+        [leaf_angle[...], level_angle[0], jnp.zeros((128 - angles, 128), F32)], axis=0
+    )
+    by_box = stacked.T
+    high = by_box.astype(BF16).astype(F32)
+    low = by_box - high
+    for to in range(16):
+        outbox[to, :points, :] = charges[:, to * 128 : (to + 1) * 128].astype(BF16)
+        pair = jnp.concatenate([high[to * 8 : to * 8 + 8], low[to * 8 : to * 8 + 8]], axis=0)
+        outbox[to, points : points + 16, :] = pair.astype(BF16)
+    own[me] = outbox[me]
+
+    def to_wide(bits):
+        to = flip(layer, bits // 4) * 4 + flip(place, bits % 4)
+        return pltpu.make_async_remote_copy(
+            src_ref=outbox.at[to],
+            dst_ref=own.at[me],
+            send_sem=wide_send.at[to],
+            recv_sem=wide_recv.at[me],
+            device_id={"wide": to},
+            device_id_type=MESH,
+        )
+
+    def from_wide(source):
+        return pltpu.make_async_remote_copy(
+            src_ref=outbox.at[source],
+            dst_ref=own.at[source],
+            send_sem=wide_send.at[source],
+            recv_sem=wide_recv.at[source],
+            device_id={"wide": source},
+            device_id_type=MESH,
+        )
+
+    def across(source):
+        return pltpu.make_async_remote_copy(
+            src_ref=own.at[source],
+            dst_ref=peer.at[source],
+            send_sem=narrow_send.at[source],
+            recv_sem=narrow_recv.at[source],
+            device_id={"narrow": other},
+            device_id_type=MESH,
+        )
+
+    switch_copy = pltpu.make_async_remote_copy(
+        src_ref=switch_angle,
+        dst_ref=peer_switch,
+        send_sem=switch_sems.at[0],
+        recv_sem=switch_sems.at[1],
+        device_id={"narrow": other},
+        device_id_type=MESH,
+    )
+
+    pl.semaphore_wait(barrier, 16)
+    across(me).start()
+    order = [1, 8, 12, 2, 9, 13, 3, 4, 10, 14, 5, 11, 15, 6, 7]
+    for bits in order:
+        to_wide(bits).start()
+    switch_copy.start()
+
+    def pass_on(group):
+        for bits in range(4):
+            if group or bits:
+                source = flip(layer, group) * 4 + flip(place, bits)
+                from_wide(source).wait_recv()
+                across(source).start()
+
+    group_columns = 4 * 128
+
+    def fill(angle, first_row, cos_to, sin_to):
+        rows = angle.shape[0]
+        both = jnp.concatenate(cos_sin(angle), axis=0)
+        halves = jnp.concatenate(split(both), axis=1)
+        for group in range(4):
+            columns = pl.ds(group * group_columns, group_columns)
+            wide = dot(halves, spread(128, group_columns, group * group_columns // per_box, per_box))
+            cos_to[pl.ds(first_row, rows), columns] = wide[:rows]
+            sin_to[pl.ds(first_row, rows), columns] = wide[rows:]
+
+    local = jnp.concatenate([switch_angle[...], level_angle[1], out_angle[...]], axis=0)
+    fill(local, 0, cos_table, sin_table)
+
+    lag_high, lag_low = split(lagrange[...])
+    leaf_matrix = jnp.concatenate([lag_high, lag_low, lag_high], axis=1)
+    eva_high, eva_low = split(evaluate[...])
+    out_matrix = jnp.concatenate([eva_high, eva_low, eva_high], axis=1)
+    both_high, both_low = split(
+        jnp.concatenate(
+            [
+                jnp.concatenate([level_self[0], level_peer[0]], axis=1),
+                jnp.concatenate([level_peer[0], level_self[0]], axis=1),
+            ],
+            axis=0,
+        )
+    )
+    swi_high, swi_low = split(switch_matrix[...])
+    swi_matrix = jnp.concatenate([swi_high, swi_low], axis=1)
+    last_high, last_low = split(jnp.concatenate([level_self[1], level_peer[1]], axis=1))
+    repeat = spread(32, group_columns, 0, per_box)
+
+    def leaf(box, base):
+        charge = jnp.concatenate([box[base + i, :points, :] for i in range(4)], axis=1).astype(F32)
+        parts = [box[base + i, points : points + 16, :].astype(F32) for i in range(4)]
+        angle = jnp.concatenate([part[:8] + part[8:] for part in parts], axis=0)
+        both = jnp.concatenate(cos_sin(angle), axis=1)
+        halves = jnp.concatenate(split(both), axis=0)
+        wide = lax.dot_general(
+            halves, repeat, (((0,), (0,)), ((), ())), preferred_element_type=F32
+        )
+        cos_part, sin_part = wide[:128], wide[128:]
+        weighted = jnp.concatenate([cos_part[:points] * charge, sin_part[:points] * charge], axis=1)
+        high, low = split(weighted)
+        state = dot(leaf_matrix, jnp.concatenate([high, high, low], axis=0))
+        turned = cos_part[points:angles], sin_part[points:angles]
+        return [state[:, :group_columns], state[:, group_columns:]], turned
+
+    def compute(group):
+        where = flip(layer, group)
+        for bits in range(4):
+            across(where * 4 + bits).wait_recv()
+        columns = pl.ds(pl.multiple_of(where * group_columns, group_columns), group_columns)
+        state_own, turn_own = leaf(own, where * 4)
+        state_peer, turn_peer = leaf(peer, where * 4)
+        state = jnp.concatenate(state_own + state_peer, axis=0).astype(BF16)
+        first = dot(both_high, state) + dot(both_low, state)
+        own_real, own_imag = turn(first[:rank], first[rank : 2 * rank], *turn_own)
+        peer_real, peer_imag = turn(first[2 * rank : 3 * rank], first[3 * rank :], *turn_peer)
+        moved = jnp.concatenate(
+            [
+                jnp.concatenate([own_real, peer_real], axis=1),
+                jnp.concatenate([own_imag, peer_imag], axis=1),
+            ],
+            axis=0,
+        ).astype(BF16)
+        middle = dot(swi_matrix, jnp.concatenate([moved, moved], axis=0))
+        own_real, own_imag = turn(
+            middle[:rank, :group_columns],
+            middle[rank:, :group_columns],
+            cos_table[:rank, columns],
+            sin_table[:rank, columns],
+        )
+        peer_real, peer_imag = turn(
+            middle[:rank, group_columns:],
+            middle[rank:, group_columns:],
+            cos_peer[:, columns],
+            sin_peer[:, columns],
+        )
+        state = jnp.concatenate([own_real, own_imag, peer_real, peer_imag], axis=0).astype(BF16)
+        last = dot(last_high, state) + dot(last_low, state)
+        real, imag = turn(
+            last[:rank],
+            last[rank:],
+            cos_table[rank : 2 * rank, columns],
+            sin_table[rank : 2 * rank, columns],
+        )
+        high, low = split(jnp.concatenate([real, imag], axis=1))
+        value = dot(out_matrix, jnp.concatenate([high, high, low], axis=0))
+        field[:, columns] = (
+            cos_table[2 * rank :, columns] * value[:, :group_columns]
+            - sin_table[2 * rank :, columns] * value[:, group_columns:]
+        ).astype(BF16)
+
+    pass_on(0)
+    pass_on(1)
+    switch_copy.wait_recv()
+    fill(peer_switch[...], 0, cos_peer, sin_peer)
+    compute(0)
+    pass_on(2)
+    compute(1)
+    pass_on(3)
+    compute(2)
+    compute(3)
+
+    for bits in range(1, 16):
+        to_wide(bits).wait_send()
+    for source in range(16):
+        across(source).wait_send()
+    switch_copy.wait_send()
+
+
+def paired_body(*operands):
+    charges, leaf_angle, lagrange = operands[:3]
+    points, columns = charges.shape
+    rank = lagrange.shape[0]
+    per_box = columns // leaf_angle.shape[1]
+    return pl.pallas_call(
+        functools.partial(kernel, per_box),
+        out_shape=jax.ShapeDtypeStruct((points, columns), BF16),
+        in_specs=[pl.BlockSpec(memory_space=pltpu.VMEM)] * len(operands),
+        out_specs=pl.BlockSpec(memory_space=pltpu.VMEM),
+        scratch_shapes=[
+            pltpu.VMEM((16, points + 16, 128), BF16),
+            pltpu.VMEM((16, points + 16, 128), BF16),
+            pltpu.VMEM((16, points + 16, 128), BF16),
+            pltpu.VMEM((rank, 128), F32),
+            pltpu.VMEM((2 * rank + points, columns), F32),
+            pltpu.VMEM((2 * rank + points, columns), F32),
+            pltpu.VMEM((rank, columns), F32),
+            pltpu.VMEM((rank, columns), F32),
+            pltpu.SemaphoreType.DMA((16,)),
+            pltpu.SemaphoreType.DMA((16,)),
+            pltpu.SemaphoreType.DMA((16,)),
+            pltpu.SemaphoreType.DMA((16,)),
+            pltpu.SemaphoreType.DMA((2,)),
+        ],
+        compiler_params=pltpu.CompilerParams(
+            collective_id=0, has_side_effects=True, vmem_limit_bytes=40 * 1024 * 1024
+        ),
+        cost_estimate=pl.CostEstimate(
+            flops=2 * 60000 * 2 * columns, bytes_accessed=4 * points * columns, transcendentals=0
+        ),
+    )(*operands)
+
+
+def fits_pairs(mesh, charges, leaf_angle, lagrange):
+    devices = mesh.shape["wide"] * mesh.shape["narrow"]
+    columns = charges.shape[1] // devices
+    boxes = leaf_angle.shape[1] // devices
+    return (
+        mesh.shape["narrow"] == 2
+        and mesh.shape["wide"] == 16
+        and columns == 2048
+        and boxes == 128
+        and charges.shape[0] % 16 == 0
+        and lagrange.shape[0] % 16 == 0
+        and charges.shape[0] + lagrange.shape[0] <= 128
+    )
+
+
 def solution(mesh):
-    return jax.shard_map(
-        body,
-        mesh=mesh,
-        in_specs=(
-            P(None, ("wide", "narrow")),
-            P(None, ("wide", "narrow")),
-            P(),
-            P(None, None, ("wide", "narrow")),
-            P(),
-            P(),
-            P(None, ("wide", "narrow")),
-            P(),
-            P(None, ("wide", "narrow")),
-            P(),
-        ),
-        out_specs=P(None, ("wide", "narrow")),
-        check_vma=False,
-    )
+    def program(charges, leaf_angle, lagrange, *rest):
+        fits = fits_pairs(mesh, charges, leaf_angle, lagrange)
+        return jax.shard_map(
+            paired_body if fits else staged_body,
+            mesh=mesh,
+            in_specs=(
+                P(None, ("wide", "narrow")),
+                P(None, ("wide", "narrow")),
+                P(),
+                P(None, None, ("wide", "narrow")),
+                P(),
+                P(),
+                P(None, ("wide", "narrow")),
+                P(),
+                P(None, ("wide", "narrow")),
+                P(),
+            ),
+            out_specs=P(None, ("wide", "narrow")),
+            check_vma=False,
+        )(charges, leaf_angle, lagrange, *rest)
+
+    return program

time: 62.4 us -> 30.6 us (0.49)
  waiting for transfers between devices: 29 us -> 0 us
  Pallas kernels: 0 us -> 21.8 us
  starting transfers between devices: 10.8 us -> 0 us
  matrix products: 8.91 us -> 0 us
  local copies, waits for them, and re-layouts: 10.5 us -> 8.14 us
  other arithmetic: 2.16 us -> 0 us
    pallas_call x0 -> x1, Pallas kernels: none -> 21.8 us  [paired_body(): pl.pallas_call(functools.partial(kernel, per_box), out_shape=jax.ShapeDty...]
    all_to_all x1 -> x0, waiting for transfers between devices: 15.8 us -> none  [body(): lax.all_to_all(boxes_state, 'wide', split_axis=1, concat_axis=1, tiled=True)]
    ppermute x2 -> x0, waiting for transfers between devices: 13.2 us -> none  [from_partner(): return lax.ppermute(value, axis, pairs)]
    dot_general x9 -> x0, matrix products: 8.91 us -> none  [product(): jnp.dot(left, right, precision=lax.Precision.HIGHEST, preferred_element_t...]
    all_to_all x1 -> x0, starting transfers between devices: 6.26 us -> none  [body(): lax.all_to_all(boxes_state, 'wide', split_axis=1, concat_axis=1, tiled=True)]
    ppermute x2 -> x0, starting transfers between devices: 4.55 us -> none  [from_partner(): return lax.ppermute(value, axis, pairs)]
    unnamed x25 -> x20, local copies, waits for them, and re-layouts: 3.82 us -> 8.14 us
    reshape x8 -> x0, local copies, waits for them, and re-layouts: 3.3 us -> none  [the longest x1 1.13 us: body(): sin_out = jnp.repeat(jnp.sin(out_angle), per_box, axis=1)]
  transfers between devices with their start and end apart: 3 -> 0, of which waited for: 3 -> 0; matrix products, arithmetic and copies ran while one was open for 12% -> 0% of each run, Pallas kernels for 0% -> 0%
where the time goes in v1:
time: 30.6 us; the launch traced here: 30 us
  Pallas kernels  21.8 us (71%)
  local copies, waits for them, and re-layouts  8.14 us (27%)
    pallas_call x1, Pallas kernels, paired_body(): pl.pallas_call(functools.partial(kernel, per_box), out_shape=jax.ShapeDty...  21.8 us
    unnamed x20, local copies, waits for them, and re-layouts  8.14 us

profile of v1, /device:TPU:0, one launch (start us, length us, event | category | flops | bytes accessed | tf_op | source)
XLA Modules:
  0.0 30.0 jit_solution(16237760366947283194)
XLA Ops:
  0.0 0.0 copy-start.3
  0.0 0.8 %copy.11.evaluate = f32[64,48]{1,0:T(8,128)S(1)} copy(f32[64,48]{0,1:T(8,128)} %param.19) | data formatting | bytes 24576 | tf_op args[9]
  0.8 0.0 copy-done.3
  0.8 0.0 copy-start
  0.8 1.0 %copy-done = f32[64,2048]{1,0:T(8,128)S(1)} copy-done((f32[64,2048]{1,0:T(8,128)S(1)}, f32[64,2048]{1,0:T(8,128)}, u32[]{:S(2)}) %copy-start) | copy-done | bytes 524312
  1.9 0.0 copy-start.1
  1.9 0.9 %copy-done.1 = f32[2,96,96]{2,1,0:T(8,128)S(1)} copy-done((f32[2,96,96]{2,1,0:T(8,128)S(1)}, f32[2,96,96]{2,1,0:T(8,128)}, u32[]{:S(2)}) %copy-start.1) | copy-done | bytes 73752
  2.8 0.0 copy-start.2
  2.8 0.9 %copy-done.2 = f32[2,96,96]{2,1,0:T(8,128)S(1)} copy-done((f32[2,96,96]{2,1,0:T(8,128)S(1)}, f32[2,96,96]{2,1,0:T(8,128)}, u32[]{:S(2)}) %copy-start.2) | copy-done | bytes 73752
  3.7 0.0 copy-start.4
  3.7 0.8 %copy-done.4 = f32[96,96]{1,0:T(8,128)S(1)} copy-done((f32[96,96]{1,0:T(8,128)S(1)}, f32[96,96]{1,0:T(8,128)}, u32[]{:S(2)}) %copy-start.4) | copy-done | bytes 36888
  4.5 0.0 copy-start.5
  4.5 0.8 %copy-done.5 = f32[64,128]{1,0:T(8,128)S(1)} copy-done((f32[64,128]{1,0:T(8,128)S(1)}, f32[64,128]{1,0:T(8,128)}, u32[]{:S(2)}) %copy-start.5) | copy-done | bytes 32792
  5.2 0.0 copy-start.6
  5.2 0.8 %copy-done.6 = f32[64,128]{1,0:T(8,128)S(1)} copy-done((f32[64,128]{1,0:T(8,128)S(1)}, f32[64,128]{1,0:T(8,128)}, u32[]{:S(2)}) %copy-start.6) | copy-done | bytes 32792
  6.0 0.0 copy-start.7
  6.0 0.7 %copy-done.7 = f32[48,64]{1,0:T(8,128)S(1)} copy-done((f32[48,64]{1,0:T(8,128)S(1)}, f32[48,64]{1,0:T(8,128)}, u32[]{:S(2)}) %copy-start.7) | copy-done | bytes 12312
  6.7 0.0 copy-start.8
  6.7 0.7 %copy-done.8 = f32[48,128]{1,0:T(8,128)S(1)} copy-done((f32[48,128]{1,0:T(8,128)S(1)}, f32[48,128]{1,0:T(8,128)}, u32[]{:S(2)}) %copy-start.8) | copy-done | bytes 24600
  7.5 21.8 %shard_map.100 = bf16[64,2048]{1,0:T(8,128)(2,1)S(1)} custom-call(f32[64,2048]{1,0:T(8,128)S(1)} %copy-done, f32[64,128]{1,0:T(8,128)S(1)} %copy-done.5, f32[48,64]{1,0:T(8,128)S(1)} %copy-done.7, f32[2,48,128]{2,1,0:T(8,128)S(1)} %copy-done.3, f32[2,96,96]{2,1,0:T(8,128)S(1)} %copy-done.1, f32[2,96,96]{2,1,0:T(8,128)S(1)} %copy-done.2, ...), custom_call_target="tpu_custom_call" | custom-call | flops 491520000 | bytes 524288 | tf_op jit(solution)/shard_map/pallas_call | solution.py:356
  29.3 0.7 %copy.13 = bf16[64,2048]{1,0:T(8,128)(2,1)} copy(bf16[64,2048]{1,0:T(8,128)(2,1)S(1)} %shard_map.100) | data formatting | bytes 524288
Async XLA Ops:
  0.0 0.8 %copy-start.3 = (f32[2,48,128]{2,1,0:T(8,128)S(1)}, f32[2,48,128]{2,1,0:T(8,128)}, u32[]{:S(2)}) copy-start(f32[2,48,128]{2,1,0:T(8,128)} %level_angle.1) | copy-start | bytes 147460
  0.8 1.0 %copy-start = (f32[64,2048]{1,0:T(8,128)S(1)}, f32[64,2048]{1,0:T(8,128)}, u32[]{:S(2)}) copy-start(f32[64,2048]{1,0:T(8,128)} %charges.1) | copy-start | bytes 1572868
  1.9 0.9 %copy-start.1 = (f32[2,96,96]{2,1,0:T(8,128)S(1)}, f32[2,96,96]{2,1,0:T(8,128)}, u32[]{:S(2)}) copy-start(f32[2,96,96]{2,1,0:T(8,128)} %level_self.1) | copy-start | bytes 221188
  2.8 0.9 %copy-start.2 = (f32[2,96,96]{2,1,0:T(8,128)S(1)}, f32[2,96,96]{2,1,0:T(8,128)}, u32[]{:S(2)}) copy-start(f32[2,96,96]{2,1,0:T(8,128)} %level_peer.1) | copy-start | bytes 221188
  3.7 0.8 %copy-start.4 = (f32[96,96]{1,0:T(8,128)S(1)}, f32[96,96]{1,0:T(8,128)}, u32[]{:S(2)}) copy-start(f32[96,96]{1,0:T(8,128)} %switch_matrix.1) | copy-start | bytes 110596
  4.5 0.8 %copy-start.5 = (f32[64,128]{1,0:T(8,128)S(1)}, f32[64,128]{1,0:T(8,128)}, u32[]{:S(2)}) copy-start(f32[64,128]{1,0:T(8,128)} %leaf_angle.1) | copy-start | bytes 98308
  5.2 0.8 %copy-start.6 = (f32[64,128]{1,0:T(8,128)S(1)}, f32[64,128]{1,0:T(8,128)}, u32[]{:S(2)}) copy-start(f32[64,128]{1,0:T(8,128)} %out_angle.1) | copy-start | bytes 98308
  6.0 0.7 %copy-start.7 = (f32[48,64]{1,0:T(8,128)S(1)}, f32[48,64]{1,0:T(8,128)}, u32[]{:S(2)}) copy-start(f32[48,64]{1,0:T(8,128)} %lagrange.1) | copy-start | bytes 36868
  6.7 0.7 %copy-start.8 = (f32[48,128]{1,0:T(8,128)S(1)}, f32[48,128]{1,0:T(8,128)}, u32[]{:S(2)}) copy-start(f32[48,128]{1,0:T(8,128)} %switch_angle.1) | copy-start | bytes 73732

commit v2 on v1

--- a/solution.py
+++ b/solution.py
@@ -130,17 +130,23 @@
 
 def kernel(
     per_box,
-    charges,
-    leaf_angle,
-    lagrange,
-    level_angle,
-    level_self,
-    level_peer,
-    switch_angle,
-    switch_matrix,
-    out_angle,
-    evaluate,
-    field,
+    *refs,
+):
+    given, refs = refs[:10], refs[10:]
+    field, (held, refs) = refs[0], (refs[1:11], refs[11:])
+    (
+        charges,
+        leaf_angle,
+        lagrange,
+        level_angle,
+        level_self,
+        level_peer,
+        switch_angle,
+        switch_matrix,
+        out_angle,
+        evaluate,
+    ) = held
+    (
     outbox,
     own,
     peer,
@@ -154,7 +160,13 @@
     narrow_send,
     narrow_recv,
     switch_sems,
-):
+    load_sems,
+    ) = refs
+    loads = [pltpu.make_async_copy(g, h, load_sems.at[i]) for i, (g, h) in enumerate(zip(given, held))]
+    first_loads = [1, 3, 0, 6]
+    later_loads = [i for i in range(10) if i not in first_loads]
+    for i in first_loads + later_loads:
+        loads[i].start()
     me = lax.axis_index("wide")
     row = lax.axis_index("narrow")
     layer = me // 4
@@ -168,6 +180,9 @@
         to = flip(layer, bits // 4) * 4 + flip(place, bits % 4)
         pl.semaphore_signal(barrier, inc=1, device_id={"wide": to}, device_id_type=MESH)
     pl.semaphore_signal(barrier, inc=1, device_id={"narrow": other}, device_id_type=MESH)
+
+    for i in first_loads:
+        loads[i].wait()
 
     stacked = jnp.concatenate(
         [leaf_angle[...], level_angle[0], jnp.zeros((128 - angles, 128), F32)], axis=0
@@ -235,6 +250,9 @@
                 from_wide(source).wait_recv()
                 across(source).start()
 
+    for i in later_loads:
+        loads[i].wait()
+
     group_columns = 4 * 128
 
     def fill(angle, first_row, cos_to, sin_to):
@@ -252,9 +270,9 @@
 
     lag_high, lag_low = split(lagrange[...])
     leaf_matrix = jnp.concatenate([lag_high, lag_low, lag_high], axis=1)
-    eva_high, eva_low = split(evaluate[...])
+    eva_high, eva_low = split(evaluate[...].T)
     out_matrix = jnp.concatenate([eva_high, eva_low, eva_high], axis=1)
-    both_high, both_low = split(
+    both_matrix = split(
         jnp.concatenate(
             [
                 jnp.concatenate([level_self[0], level_peer[0]], axis=1),
@@ -263,9 +281,11 @@
             axis=0,
         )
     )
+    both_matrix = jnp.concatenate(both_matrix, axis=0)
     swi_high, swi_low = split(switch_matrix[...])
     swi_matrix = jnp.concatenate([swi_high, swi_low], axis=1)
-    last_high, last_low = split(jnp.concatenate([level_self[1], level_peer[1]], axis=1))
+    last_matrix = split(jnp.concatenate([level_self[1], level_peer[1]], axis=1))
+    last_matrix = jnp.concatenate(last_matrix, axis=0)
     repeat = spread(32, group_columns, 0, per_box)
 
     def leaf(box, base):
@@ -286,13 +306,14 @@
 
     def compute(group):
         where = flip(layer, group)
+        columns = pl.ds(pl.multiple_of(where * group_columns, group_columns), group_columns)
+        state_own, turn_own = leaf(own, where * 4)
         for bits in range(4):
             across(where * 4 + bits).wait_recv()
-        columns = pl.ds(pl.multiple_of(where * group_columns, group_columns), group_columns)
-        state_own, turn_own = leaf(own, where * 4)
         state_peer, turn_peer = leaf(peer, where * 4)
         state = jnp.concatenate(state_own + state_peer, axis=0).astype(BF16)
-        first = dot(both_high, state) + dot(both_low, state)
+        first = dot(both_matrix, state)
+        first = first[: 4 * rank] + first[4 * rank :]
         own_real, own_imag = turn(first[:rank], first[rank : 2 * rank], *turn_own)
         peer_real, peer_imag = turn(first[2 * rank : 3 * rank], first[3 * rank :], *turn_peer)
         moved = jnp.concatenate(
@@ -316,7 +337,8 @@
             sin_peer[:, columns],
         )
         state = jnp.concatenate([own_real, own_imag, peer_real, peer_imag], axis=0).astype(BF16)
-        last = dot(last_high, state) + dot(last_low, state)
+        last = dot(last_matrix, state)
+        last = last[: 2 * rank] + last[2 * rank :]
         real, imag = turn(
             last[:rank],
             last[rank:],
@@ -353,12 +375,14 @@
     points, columns = charges.shape
     rank = lagrange.shape[0]
     per_box = columns // leaf_angle.shape[1]
+    operands = operands[:-1] + (operands[-1].T,)
     return pl.pallas_call(
         functools.partial(kernel, per_box),
         out_shape=jax.ShapeDtypeStruct((points, columns), BF16),
-        in_specs=[pl.BlockSpec(memory_space=pltpu.VMEM)] * len(operands),
+        in_specs=[pl.BlockSpec(memory_space=pltpu.HBM)] * len(operands),
         out_specs=pl.BlockSpec(memory_space=pltpu.VMEM),
-        scratch_shapes=[
+        scratch_shapes=[pltpu.VMEM(operand.shape, F32) for operand in operands]
+        + [
             pltpu.VMEM((16, points + 16, 128), BF16),
             pltpu.VMEM((16, points + 16, 128), BF16),
             pltpu.VMEM((16, points + 16, 128), BF16),
@@ -372,9 +396,10 @@
             pltpu.SemaphoreType.DMA((16,)),
             pltpu.SemaphoreType.DMA((16,)),
             pltpu.SemaphoreType.DMA((2,)),
+            pltpu.SemaphoreType.DMA((len(operands),)),
         ],
         compiler_params=pltpu.CompilerParams(
-            collective_id=0, has_side_effects=True, vmem_limit_bytes=40 * 1024 * 1024
+            collective_id=0, has_side_effects=True, vmem_limit_bytes=60 * 1024 * 1024
         ),
         cost_estimate=pl.CostEstimate(
             flops=2 * 60000 * 2 * columns, bytes_accessed=4 * points * columns, transcendentals=0

time: 30.6 us -> 24.4 us (0.80); the launches traced: 30 us -> 24.3 us
  local copies, waits for them, and re-layouts: 8.14 us -> 1.67 us
  Pallas kernels: 21.8 us -> 22.6 us
    unnamed x20 -> x1, local copies, waits for them, and re-layouts: 8.14 us -> 1.67 us
    pallas_call x1, Pallas kernels: 21.8 us -> 22.6 us  [paired_body(): pl.pallas_call(functools.partial(kernel, per_box), out_shape=jax.ShapeDty...]
where the time goes in v2:
time: 24.4 us; the launch traced here: 24.3 us
  Pallas kernels  22.6 us (93%)
  local copies, waits for them, and re-layouts  1.67 us (7%)
    pallas_call x1, Pallas kernels, paired_body(): pl.pallas_call(functools.partial(kernel, per_box), out_shape=jax.ShapeDty...  22.6 us
    unnamed x1, local copies, waits for them, and re-layouts  1.67 us

profile of v2, /device:TPU:0, one launch (start us, length us, event | category | flops | bytes accessed | tf_op | source)
XLA Modules:
  0.0 24.3 jit_solution(12825929098914811408)
XLA Ops:
  0.0 22.6 %shard_map.100 = bf16[64,2048]{1,0:T(8,128)(2,1)} custom-call(f32[64,2048]{1,0:T(8,128)} %refs_0_.1, f32[64,128]{1,0:T(8,128)} %refs_1_.1, f32[48,64]{1,0:T(8,128)} %refs_2_.1, f32[2,48,128]{2,1,0:T(8,128)} %refs_3_.1, f32[2,96,96]{2,1,0:T(8,128)} %refs_4_.1, f32[2,96,96]{2,1,0:T(8,128)} %refs_5_.1, f32[48,128]{1,0:T(8,128)} %refs_6_.1, f32[96,96]{1,0:T(8,128)} %refs_7_.1, ...), custom_call_target="tpu_custom_call" | custom-call | flops 491520000 | bytes 524288 | tf_op jit(solution)/shard_map/pallas_call | solution.py:379
  22.6 1.7 %copy.12 = bf16[64,2048]{1,0:T(8,128)(2,1)} copy(bf16[64,2048]{1,0:T(8,128)(2,1)} %shard_map.100) | data formatting | bytes 524288

commit v3 on v2

--- a/solution.py
+++ b/solution.py
@@ -243,8 +243,8 @@
         to_wide(bits).start()
     switch_copy.start()
 
-    def pass_on(group):
-        for bits in range(4):
+    def pass_on(group, half):
+        for bits in (2 * half, 2 * half + 1):
             if group or bits:
                 source = flip(layer, group) * 4 + flip(place, bits)
                 from_wide(source).wait_recv()
@@ -253,15 +253,16 @@
     for i in later_loads:
         loads[i].wait()
 
-    group_columns = 4 * 128
+    fill_columns = 4 * 128
+    group_columns = 2 * 128
 
     def fill(angle, first_row, cos_to, sin_to):
         rows = angle.shape[0]
         both = jnp.concatenate(cos_sin(angle), axis=0)
         halves = jnp.concatenate(split(both), axis=1)
         for group in range(4):
-            columns = pl.ds(group * group_columns, group_columns)
-            wide = dot(halves, spread(128, group_columns, group * group_columns // per_box, per_box))
+            columns = pl.ds(group * fill_columns, fill_columns)
+            wide = dot(halves, spread(128, fill_columns, group * fill_columns // per_box, per_box))
             cos_to[pl.ds(first_row, rows), columns] = wide[:rows]
             sin_to[pl.ds(first_row, rows), columns] = wide[rows:]
 
@@ -269,7 +270,7 @@
     fill(local, 0, cos_table, sin_table)
 
     lag_high, lag_low = split(lagrange[...])
-    leaf_matrix = jnp.concatenate([lag_high, lag_low, lag_high], axis=1)
+    leaf_matrix = jnp.concatenate([lag_high, lag_low], axis=1)
     eva_high, eva_low = split(evaluate[...].T)
     out_matrix = jnp.concatenate([eva_high, eva_low, eva_high], axis=1)
     both_matrix = split(
@@ -286,11 +287,11 @@
     swi_matrix = jnp.concatenate([swi_high, swi_low], axis=1)
     last_matrix = split(jnp.concatenate([level_self[1], level_peer[1]], axis=1))
     last_matrix = jnp.concatenate(last_matrix, axis=0)
-    repeat = spread(32, group_columns, 0, per_box)
+    repeat = spread(16, group_columns, 0, per_box)
 
     def leaf(box, base):
-        charge = jnp.concatenate([box[base + i, :points, :] for i in range(4)], axis=1).astype(F32)
-        parts = [box[base + i, points : points + 16, :].astype(F32) for i in range(4)]
+        charge = jnp.concatenate([box[base + i, :points, :] for i in range(2)], axis=1).astype(F32)
+        parts = [box[base + i, points : points + 16, :].astype(F32) for i in range(2)]
         angle = jnp.concatenate([part[:8] + part[8:] for part in parts], axis=0)
         both = jnp.concatenate(cos_sin(angle), axis=1)
         halves = jnp.concatenate(split(both), axis=0)
@@ -299,18 +300,18 @@
         )
         cos_part, sin_part = wide[:128], wide[128:]
         weighted = jnp.concatenate([cos_part[:points] * charge, sin_part[:points] * charge], axis=1)
-        high, low = split(weighted)
-        state = dot(leaf_matrix, jnp.concatenate([high, high, low], axis=0))
+        weighted = weighted.astype(BF16)
+        state = dot(leaf_matrix, jnp.concatenate([weighted, weighted], axis=0))
         turned = cos_part[points:angles], sin_part[points:angles]
         return [state[:, :group_columns], state[:, group_columns:]], turned
 
-    def compute(group):
-        where = flip(layer, group)
-        columns = pl.ds(pl.multiple_of(where * group_columns, group_columns), group_columns)
-        state_own, turn_own = leaf(own, where * 4)
-        for bits in range(4):
-            across(where * 4 + bits).wait_recv()
-        state_peer, turn_peer = leaf(peer, where * 4)
+    def compute(group, half):
+        base = flip(layer, group) * 4 + flip(place // 2, half) * 2
+        columns = pl.ds(pl.multiple_of(base * 128, group_columns), group_columns)
+        state_own, turn_own = leaf(own, base)
+        for i in range(2):
+            across(base + i).wait_recv()
+        state_peer, turn_peer = leaf(peer, base)
         state = jnp.concatenate(state_own + state_peer, axis=0).astype(BF16)
         first = dot(both_matrix, state)
         first = first[: 4 * rank] + first[4 * rank :]
@@ -352,16 +353,24 @@
             - sin_table[2 * rank :, columns] * value[:, group_columns:]
         ).astype(BF16)
 
-    pass_on(0)
-    pass_on(1)
+    pass_on(0, 0)
+    pass_on(0, 1)
+    pass_on(1, 0)
+    pass_on(1, 1)
     switch_copy.wait_recv()
     fill(peer_switch[...], 0, cos_peer, sin_peer)
-    compute(0)
-    pass_on(2)
-    compute(1)
-    pass_on(3)
-    compute(2)
-    compute(3)
+    compute(0, 0)
+    pass_on(2, 0)
+    compute(0, 1)
+    pass_on(3, 0)
+    compute(1, 0)
+    pass_on(2, 1)
+    compute(1, 1)
+    pass_on(3, 1)
+    compute(2, 0)
+    compute(3, 0)
+    compute(2, 1)
+    compute(3, 1)
 
     for bits in range(1, 16):
         to_wide(bits).wait_send()
@@ -378,7 +387,7 @@
     operands = operands[:-1] + (operands[-1].T,)
     return pl.pallas_call(
         functools.partial(kernel, per_box),
-        out_shape=jax.ShapeDtypeStruct((points, columns), BF16),
+        out_shape=pltpu.VMEM((points, columns), BF16),
         in_specs=[pl.BlockSpec(memory_space=pltpu.HBM)] * len(operands),
         out_specs=pl.BlockSpec(memory_space=pltpu.VMEM),
         scratch_shapes=[pltpu.VMEM(operand.shape, F32) for operand in operands]
@@ -399,7 +408,7 @@
             pltpu.SemaphoreType.DMA((len(operands),)),
         ],
         compiler_params=pltpu.CompilerParams(
-            collective_id=0, has_side_effects=True, vmem_limit_bytes=60 * 1024 * 1024
+            collective_id=0, has_side_effects=True, vmem_limit_bytes=58 * 1024 * 1024
         ),
         cost_estimate=pl.CostEstimate(
             flops=2 * 60000 * 2 * columns, bytes_accessed=4 * points * columns, transcendentals=0

time: 24.4 us -> 24.6 us (level)
  the two profiles are of different devices: /device:TPU:0 before, /device:TPU:15 now
where the time goes in v3:
time: 24.6 us; the launch traced here: 24.5 us
  Pallas kernels  23.8 us (97%)
  local copies, waits for them, and re-layouts  0.71 us (3%)
    pallas_call x1, Pallas kernels, paired_body(): pl.pallas_call(functools.partial(kernel, per_box), out_shape=pltpu.VMEM((...  23.8 us
    unnamed x1, local copies, waits for them, and re-layouts  0.71 us

profile of v3, /device:TPU:15, one launch (start us, length us, event | category | flops | bytes accessed | tf_op | source)
XLA Modules:
  0.0 24.5 jit_solution(15978436076569100039)
XLA Ops:
  0.0 23.8 %shard_map.100 = bf16[64,2048]{1,0:T(8,128)(2,1)S(1)} custom-call(f32[64,2048]{1,0:T(8,128)} %refs_0_.1, f32[64,128]{1,0:T(8,128)} %refs_1_.1, f32[48,64]{1,0:T(8,128)} %refs_2_.1, f32[2,48,128]{2,1,0:T(8,128)} %refs_3_.1, f32[2,96,96]{2,1,0:T(8,128)} %refs_4_.1, f32[2,96,96]{2,1,0:T(8,128)} %refs_5_.1, f32[48,128]{1,0:T(8,128)} %refs_6_.1, ...), custom_call_target="tpu_custom_call" | custom-call | flops 491520000 | bytes 524288 | tf_op jit(solution)/shard_map/pallas_call | solution.py:388
  23.8 0.7 %copy.12 = bf16[64,2048]{1,0:T(8,128)(2,1)} copy(bf16[64,2048]{1,0:T(8,128)(2,1)S(1)} %shard_map.100) | data formatting | bytes 524288

commit v4 on v2

--- a/solution.py
+++ b/solution.py
@@ -238,7 +238,7 @@
 
     pl.semaphore_wait(barrier, 16)
     across(me).start()
-    order = [1, 8, 12, 2, 9, 13, 3, 4, 10, 14, 5, 11, 15, 6, 7]
+    order = [1, 8, 2, 9, 4, 10, 3, 11, 5, 12, 6, 13, 7, 14, 15]
     for bits in order:
         to_wide(bits).start()
     switch_copy.start()
@@ -253,15 +253,16 @@
     for i in later_loads:
         loads[i].wait()
 
-    group_columns = 4 * 128
+    fill_columns = 4 * 128
+    group_columns = 8 * 128
 
     def fill(angle, first_row, cos_to, sin_to):
         rows = angle.shape[0]
         both = jnp.concatenate(cos_sin(angle), axis=0)
         halves = jnp.concatenate(split(both), axis=1)
         for group in range(4):
-            columns = pl.ds(group * group_columns, group_columns)
-            wide = dot(halves, spread(128, group_columns, group * group_columns // per_box, per_box))
+            columns = pl.ds(group * fill_columns, fill_columns)
+            wide = dot(halves, spread(128, fill_columns, group * fill_columns // per_box, per_box))
             cos_to[pl.ds(first_row, rows), columns] = wide[:rows]
             sin_to[pl.ds(first_row, rows), columns] = wide[rows:]
 
@@ -269,7 +270,7 @@
     fill(local, 0, cos_table, sin_table)
 
     lag_high, lag_low = split(lagrange[...])
-    leaf_matrix = jnp.concatenate([lag_high, lag_low, lag_high], axis=1)
+    leaf_matrix = jnp.concatenate([lag_high, lag_low], axis=1)
     eva_high, eva_low = split(evaluate[...].T)
     out_matrix = jnp.concatenate([eva_high, eva_low, eva_high], axis=1)
     both_matrix = split(
@@ -286,11 +287,11 @@
     swi_matrix = jnp.concatenate([swi_high, swi_low], axis=1)
     last_matrix = split(jnp.concatenate([level_self[1], level_peer[1]], axis=1))
     last_matrix = jnp.concatenate(last_matrix, axis=0)
-    repeat = spread(32, group_columns, 0, per_box)
-
-    def leaf(box, base):
-        charge = jnp.concatenate([box[base + i, :points, :] for i in range(4)], axis=1).astype(F32)
-        parts = [box[base + i, points : points + 16, :].astype(F32) for i in range(4)]
+    repeat = spread(64, group_columns, 0, per_box)
+
+    def leaf(box, sources):
+        charge = jnp.concatenate([box[source, :points, :] for source in sources], axis=1).astype(F32)
+        parts = [box[source, points : points + 16, :].astype(F32) for source in sources]
         angle = jnp.concatenate([part[:8] + part[8:] for part in parts], axis=0)
         both = jnp.concatenate(cos_sin(angle), axis=1)
         halves = jnp.concatenate(split(both), axis=0)
@@ -299,18 +300,25 @@
         )
         cos_part, sin_part = wide[:128], wide[128:]
         weighted = jnp.concatenate([cos_part[:points] * charge, sin_part[:points] * charge], axis=1)
-        high, low = split(weighted)
-        state = dot(leaf_matrix, jnp.concatenate([high, high, low], axis=0))
+        weighted = weighted.astype(BF16)
+        state = dot(leaf_matrix, jnp.concatenate([weighted, weighted], axis=0))
         turned = cos_part[points:angles], sin_part[points:angles]
         return [state[:, :group_columns], state[:, group_columns:]], turned
 
-    def compute(group):
-        where = flip(layer, group)
-        columns = pl.ds(pl.multiple_of(where * group_columns, group_columns), group_columns)
-        state_own, turn_own = leaf(own, where * 4)
-        for bits in range(4):
-            across(where * 4 + bits).wait_recv()
-        state_peer, turn_peer = leaf(peer, where * 4)
+    def compute(groups):
+        wheres = [flip(layer, group) for group in groups]
+        sources = [where * 4 + i for where in wheres for i in range(4)]
+        blocks = [pl.ds(pl.multiple_of(where * 512, 512), 512) for where in wheres]
+
+        def table(values, start, rows):
+            return jnp.concatenate(
+                [values[start : start + rows, block] for block in blocks], axis=1
+            )
+
+        state_own, turn_own = leaf(own, sources)
+        for source in sources:
+            across(source).wait_recv()
+        state_peer, turn_peer = leaf(peer, sources)
         state = jnp.concatenate(state_own + state_peer, axis=0).astype(BF16)
         first = dot(both_matrix, state)
         first = first[: 4 * rank] + first[4 * rank :]
@@ -327,14 +335,14 @@
         own_real, own_imag = turn(
             middle[:rank, :group_columns],
             middle[rank:, :group_columns],
-            cos_table[:rank, columns],
-            sin_table[:rank, columns],
+            table(cos_table, 0, rank),
+            table(sin_table, 0, rank),
         )
         peer_real, peer_imag = turn(
             middle[:rank, group_columns:],
             middle[rank:, group_columns:],
-            cos_peer[:, columns],
-            sin_peer[:, columns],
+            table(cos_peer, 0, rank),
+            table(sin_peer, 0, rank),
         )
         state = jnp.concatenate([own_real, own_imag, peer_real, peer_imag], axis=0).astype(BF16)
         last = dot(last_matrix, state)
@@ -342,26 +350,26 @@
         real, imag = turn(
             last[:rank],
             last[rank:],
-            cos_table[rank : 2 * rank, columns],
-            sin_table[rank : 2 * rank, columns],
+            table(cos_table, rank, rank),
+            table(sin_table, rank, rank),
         )
         high, low = split(jnp.concatenate([real, imag], axis=1))
         value = dot(out_matrix, jnp.concatenate([high, high, low], axis=0))
-        field[:, columns] = (
-            cos_table[2 * rank :, columns] * value[:, :group_columns]
-            - sin_table[2 * rank :, columns] * value[:, group_columns:]
+        result = (
+            table(cos_table, 2 * rank, points) * value[:, :group_columns]
+            - table(sin_table, 2 * rank, points) * value[:, group_columns:]
         ).astype(BF16)
+        for i, block in enumerate(blocks):
+            field[:, block] = result[:, i * 512 : (i + 1) * 512]
 
     pass_on(0)
     pass_on(1)
     switch_copy.wait_recv()
     fill(peer_switch[...], 0, cos_peer, sin_peer)
-    compute(0)
     pass_on(2)
-    compute(1)
+    compute((0, 1))
     pass_on(3)
-    compute(2)
-    compute(3)
+    compute((2, 3))
 
     for bits in range(1, 16):
         to_wide(bits).wait_send()
@@ -378,7 +386,7 @@
     operands = operands[:-1] + (operands[-1].T,)
     return pl.pallas_call(
         functools.partial(kernel, per_box),
-        out_shape=jax.ShapeDtypeStruct((points, columns), BF16),
+        out_shape=pltpu.VMEM((points, columns), BF16),
         in_specs=[pl.BlockSpec(memory_space=pltpu.HBM)] * len(operands),
         out_specs=pl.BlockSpec(memory_space=pltpu.VMEM),
         scratch_shapes=[pltpu.VMEM(operand.shape, F32) for operand in operands]
@@ -399,7 +407,7 @@
             pltpu.SemaphoreType.DMA((len(operands),)),
         ],
         compiler_params=pltpu.CompilerParams(
-            collective_id=0, has_side_effects=True, vmem_limit_bytes=60 * 1024 * 1024
+            collective_id=0, has_side_effects=True, vmem_limit_bytes=58 * 1024 * 1024
         ),
         cost_estimate=pl.CostEstimate(
             flops=2 * 60000 * 2 * columns, bytes_accessed=4 * points * columns, transcendentals=0

time: 24.4 us -> 22.2 us (0.910)
  Pallas kernels: 22.6 us -> 21.3 us
  local copies, waits for them, and re-layouts: 1.67 us -> 0.71 us
    pallas_call x1, Pallas kernels: 22.6 us -> 21.3 us  [paired_body(): pl.pallas_call(functools.partial(kernel, per_box), out_shape=pltpu.VMEM((...]
    unnamed x1, local copies, waits for them, and re-layouts: 1.67 us -> 0.71 us
where the time goes in v4:
time: 22.2 us; the launch traced here: 22.1 us
  Pallas kernels  21.3 us (96%)
  local copies, waits for them, and re-layouts  0.71 us (3%)
    pallas_call x1, Pallas kernels, paired_body(): pl.pallas_call(functools.partial(kernel, per_box), out_shape=pltpu.VMEM((...  21.3 us
    unnamed x1, local copies, waits for them, and re-layouts  0.71 us

profile of v4, /device:TPU:0, one launch (start us, length us, event | category | flops | bytes accessed | tf_op | source)
XLA Modules:
  0.0 22.1 jit_solution(2316764153949824963)
XLA Ops:
  0.0 21.3 %shard_map.100 = bf16[64,2048]{1,0:T(8,128)(2,1)S(1)} custom-call(f32[64,2048]{1,0:T(8,128)} %refs_0_.1, f32[64,128]{1,0:T(8,128)} %refs_1_.1, f32[48,64]{1,0:T(8,128)} %refs_2_.1, f32[2,48,128]{2,1,0:T(8,128)} %refs_3_.1, f32[2,96,96]{2,1,0:T(8,128)} %refs_4_.1, f32[2,96,96]{2,1,0:T(8,128)} %refs_5_.1, f32[48,128]{1,0:T(8,128)} %refs_6_.1, ...), custom_call_target="tpu_custom_call" | custom-call | flops 491520000 | bytes 524288 | tf_op jit(solution)/shard_map/pallas_call | solution.py:387
  21.3 0.7 %copy.12 = bf16[64,2048]{1,0:T(8,128)(2,1)} copy(bf16[64,2048]{1,0:T(8,128)(2,1)S(1)} %shard_map.100) | data formatting | bytes 524288

commit v5 on v4

--- a/solution.py
+++ b/solution.py
@@ -254,7 +254,6 @@
         loads[i].wait()
 
     fill_columns = 4 * 128
-    group_columns = 8 * 128
 
     def fill(angle, first_row, cos_to, sin_to):
         rows = angle.shape[0]
@@ -266,8 +265,6 @@
             cos_to[pl.ds(first_row, rows), columns] = wide[:rows]
             sin_to[pl.ds(first_row, rows), columns] = wide[rows:]
 
-    local = jnp.concatenate([switch_angle[...], level_angle[1], out_angle[...]], axis=0)
-    fill(local, 0, cos_table, sin_table)
 
     lag_high, lag_low = split(lagrange[...])
     leaf_matrix = jnp.concatenate([lag_high, lag_low], axis=1)
@@ -287,9 +284,10 @@
     swi_matrix = jnp.concatenate([swi_high, swi_low], axis=1)
     last_matrix = split(jnp.concatenate([level_self[1], level_peer[1]], axis=1))
     last_matrix = jnp.concatenate(last_matrix, axis=0)
-    repeat = spread(64, group_columns, 0, per_box)
 
     def leaf(box, sources):
+        group_columns = 128 * len(sources)
+        repeat = spread(8 * len(sources), group_columns, 0, per_box)
         charge = jnp.concatenate([box[source, :points, :] for source in sources], axis=1).astype(F32)
         parts = [box[source, points : points + 16, :].astype(F32) for source in sources]
         angle = jnp.concatenate([part[:8] + part[8:] for part in parts], axis=0)
@@ -305,7 +303,8 @@
         turned = cos_part[points:angles], sin_part[points:angles]
         return [state[:, :group_columns], state[:, group_columns:]], turned
 
-    def compute(groups):
+    def compute(groups, meanwhile=None):
+        group_columns = 512 * len(groups)
         wheres = [flip(layer, group) for group in groups]
         sources = [where * 4 + i for where in wheres for i in range(4)]
         blocks = [pl.ds(pl.multiple_of(where * 512, 512), 512) for where in wheres]
@@ -316,6 +315,8 @@
             )
 
         state_own, turn_own = leaf(own, sources)
+        if meanwhile is not None:
+            pass_on(meanwhile)
         for source in sources:
             across(source).wait_recv()
         state_peer, turn_peer = leaf(peer, sources)
@@ -363,13 +364,14 @@
             field[:, block] = result[:, i * 512 : (i + 1) * 512]
 
     pass_on(0)
+    local = jnp.concatenate([switch_angle[...], level_angle[1], out_angle[...]], axis=0)
+    fill(local, 0, cos_table, sin_table)
     pass_on(1)
     switch_copy.wait_recv()
     fill(peer_switch[...], 0, cos_peer, sin_peer)
-    pass_on(2)
-    compute((0, 1))
-    pass_on(3)
-    compute((2, 3))
+    compute((0, 1), 2)
+    compute((2,), 3)
+    compute((3,))
 
     for bits in range(1, 16):
         to_wide(bits).wait_send()

time: 22.2 us -> 21.9 us (0.986)
  Pallas kernels: 21.3 us -> 21 us
    pallas_call x1, Pallas kernels: 21.3 us -> 21 us  [paired_body(): pl.pallas_call(functools.partial(kernel, per_box), out_shape=pltpu.VMEM((...]
where the time goes in v5:
time: 21.9 us; the launch traced here: 21.7 us
  Pallas kernels  21 us (96%)
  local copies, waits for them, and re-layouts  0.71 us (3%)
    pallas_call x1, Pallas kernels, paired_body(): pl.pallas_call(functools.partial(kernel, per_box), out_shape=pltpu.VMEM((...  21 us
    unnamed x1, local copies, waits for them, and re-layouts  0.71 us

profile of v5, /device:TPU:0, one launch (start us, length us, event | category | flops | bytes accessed | tf_op | source)
XLA Modules:
  0.0 21.7 jit_solution(17815187178455889184)
XLA Ops:
  0.0 21.0 %shard_map.100 = bf16[64,2048]{1,0:T(8,128)(2,1)S(1)} custom-call(f32[64,2048]{1,0:T(8,128)} %refs_0_.1, f32[64,128]{1,0:T(8,128)} %refs_1_.1, f32[48,64]{1,0:T(8,128)} %refs_2_.1, f32[2,48,128]{2,1,0:T(8,128)} %refs_3_.1, f32[2,96,96]{2,1,0:T(8,128)} %refs_4_.1, f32[2,96,96]{2,1,0:T(8,128)} %refs_5_.1, f32[48,128]{1,0:T(8,128)} %refs_6_.1, ...), custom_call_target="tpu_custom_call" | custom-call | flops 491520000 | bytes 524288 | tf_op jit(solution)/shard_map/pallas_call | solution.py:389
  21.0 0.7 %copy.12 = bf16[64,2048]{1,0:T(8,128)(2,1)} copy(bf16[64,2048]{1,0:T(8,128)(2,1)S(1)} %shard_map.100) | data formatting | bytes 524288

commit v6 on v5

--- a/solution.py
+++ b/solution.py
@@ -238,9 +238,11 @@
 
     pl.semaphore_wait(barrier, 16)
     across(me).start()
-    order = [1, 8, 2, 9, 4, 10, 3, 11, 5, 12, 6, 13, 7, 14, 15]
-    for bits in order:
-        to_wide(bits).start()
+    def send(order):
+        for bits in order:
+            to_wide(bits).start()
+
+    send([1, 8, 2, 9, 3, 10, 4, 11, 5])
     switch_copy.start()
 
     def pass_on(group):
@@ -364,9 +366,11 @@
             field[:, block] = result[:, i * 512 : (i + 1) * 512]
 
     pass_on(0)
+    send([6, 12, 7, 13])
     local = jnp.concatenate([switch_angle[...], level_angle[1], out_angle[...]], axis=0)
     fill(local, 0, cos_table, sin_table)
     pass_on(1)
+    send([14, 15])
     switch_copy.wait_recv()
     fill(peer_switch[...], 0, cos_peer, sin_peer)
     compute((0, 1), 2)

time: 21.9 us -> 23.5 us (1.073)
  Pallas kernels: 21 us -> 22.7 us
    pallas_call x1, Pallas kernels: 21 us -> 22.7 us  [paired_body(): pl.pallas_call(functools.partial(kernel, per_box), out_shape=pltpu.VMEM((...]
where the time goes in v6:
time: 23.5 us; the launch traced here: 23.4 us
  Pallas kernels  22.7 us (97%)
  local copies, waits for them, and re-layouts  0.71 us (3%)
    pallas_call x1, Pallas kernels, paired_body(): pl.pallas_call(functools.partial(kernel, per_box), out_shape=pltpu.VMEM((...  22.7 us
    unnamed x1, local copies, waits for them, and re-layouts  0.71 us

profile of v6, /device:TPU:0, one launch (start us, length us, event | category | flops | bytes accessed | tf_op | source)
XLA Modules:
  0.0 23.4 jit_solution(13951306700804898506)
XLA Ops:
  0.0 22.7 %shard_map.100 = bf16[64,2048]{1,0:T(8,128)(2,1)S(1)} custom-call(f32[64,2048]{1,0:T(8,128)} %refs_0_.1, f32[64,128]{1,0:T(8,128)} %refs_1_.1, f32[48,64]{1,0:T(8,128)} %refs_2_.1, f32[2,48,128]{2,1,0:T(8,128)} %refs_3_.1, f32[2,96,96]{2,1,0:T(8,128)} %refs_4_.1, f32[2,96,96]{2,1,0:T(8,128)} %refs_5_.1, f32[48,128]{1,0:T(8,128)} %refs_6_.1, ...), custom_call_target="tpu_custom_call" | custom-call | flops 491520000 | bytes 524288 | tf_op jit(solution)/shard_map/pallas_call | solution.py:393
  22.7 0.7 %copy.12 = bf16[64,2048]{1,0:T(8,128)(2,1)} copy(bf16[64,2048]{1,0:T(8,128)(2,1)S(1)} %shard_map.100) | data formatting | bytes 524288

commit v7 on v5

--- a/solution.py
+++ b/solution.py
@@ -237,10 +237,10 @@
     )
 
     pl.semaphore_wait(barrier, 16)
-    across(me).start()
-    order = [1, 8, 2, 9, 4, 10, 3, 11, 5, 12, 6, 13, 7, 14, 15]
+    order = [8, 9, 1, 10, 11, 2, 12, 4, 13, 3, 14, 5, 15, 6, 7]
     for bits in order:
         to_wide(bits).start()
+    across(me).start()
     switch_copy.start()
 
     def pass_on(group):

time: 21.9 us -> 22.5 us (1.027)
  the two profiles are of different devices: /device:TPU:0 before, /device:TPU:12 now
where the time goes in v7:
time: 22.5 us; the launch traced here: 22.3 us
  Pallas kernels  21.6 us (96%)
  local copies, waits for them, and re-layouts  0.71 us (3%)
    pallas_call x1, Pallas kernels, paired_body(): pl.pallas_call(functools.partial(kernel, per_box), out_shape=pltpu.VMEM((...  21.6 us
    unnamed x1, local copies, waits for them, and re-layouts  0.71 us

profile of v7, /device:TPU:12, one launch (start us, length us, event | category | flops | bytes accessed | tf_op | source)
XLA Modules:
  0.0 22.3 jit_solution(10813142171007369283)
XLA Ops:
  0.0 21.6 %shard_map.100 = bf16[64,2048]{1,0:T(8,128)(2,1)S(1)} custom-call(f32[64,2048]{1,0:T(8,128)} %refs_0_.1, f32[64,128]{1,0:T(8,128)} %refs_1_.1, f32[48,64]{1,0:T(8,128)} %refs_2_.1, f32[2,48,128]{2,1,0:T(8,128)} %refs_3_.1, f32[2,96,96]{2,1,0:T(8,128)} %refs_4_.1, f32[2,96,96]{2,1,0:T(8,128)} %refs_5_.1, f32[48,128]{1,0:T(8,128)} %refs_6_.1, ...), custom_call_target="tpu_custom_call" | custom-call | flops 491520000 | bytes 524288 | tf_op jit(solution)/shard_map/pallas_call | solution.py:389
  21.6 0.7 %copy.12 = bf16[64,2048]{1,0:T(8,128)(2,1)} copy(bf16[64,2048]{1,0:T(8,128)(2,1)S(1)} %shard_map.100) | data formatting | bytes 524288

commit v8 on v5

--- a/solution.py
+++ b/solution.py
@@ -279,11 +279,11 @@
             axis=0,
         )
     )
-    both_matrix = jnp.concatenate(both_matrix, axis=0)
+    both_matrix = jnp.concatenate(both_matrix, axis=1)
     swi_high, swi_low = split(switch_matrix[...])
     swi_matrix = jnp.concatenate([swi_high, swi_low], axis=1)
     last_matrix = split(jnp.concatenate([level_self[1], level_peer[1]], axis=1))
-    last_matrix = jnp.concatenate(last_matrix, axis=0)
+    last_matrix = jnp.concatenate(last_matrix, axis=1)
 
     def leaf(box, sources):
         group_columns = 128 * len(sources)
@@ -321,8 +321,7 @@
             across(source).wait_recv()
         state_peer, turn_peer = leaf(peer, sources)
         state = jnp.concatenate(state_own + state_peer, axis=0).astype(BF16)
-        first = dot(both_matrix, state)
-        first = first[: 4 * rank] + first[4 * rank :]
+        first = dot(both_matrix, jnp.concatenate([state, state], axis=0))
         own_real, own_imag = turn(first[:rank], first[rank : 2 * rank], *turn_own)
         peer_real, peer_imag = turn(first[2 * rank : 3 * rank], first[3 * rank :], *turn_peer)
         moved = jnp.concatenate(
@@ -346,8 +345,7 @@
             table(sin_peer, 0, rank),
         )
         state = jnp.concatenate([own_real, own_imag, peer_real, peer_imag], axis=0).astype(BF16)
-        last = dot(last_matrix, state)
-        last = last[: 2 * rank] + last[2 * rank :]
+        last = dot(last_matrix, jnp.concatenate([state, state], axis=0))
         real, imag = turn(
             last[:rank],
             last[rank:],

time: 21.9 us -> 21.9 us (level)
  no operation moved by 1% of the time
where the time goes in v8:
time: 21.9 us; the launch traced here: 21.8 us
  Pallas kernels  21 us (96%)
  local copies, waits for them, and re-layouts  0.71 us (3%)
    pallas_call x1, Pallas kernels, paired_body(): pl.pallas_call(functools.partial(kernel, per_box), out_shape=pltpu.VMEM((...  21 us
    unnamed x1, local copies, waits for them, and re-layouts  0.71 us

profile of v8, /device:TPU:0, one launch (start us, length us, event | category | flops | bytes accessed | tf_op | source)
XLA Modules:
  0.0 21.8 jit_solution(1974660571209934389)
XLA Ops:
  0.0 21.0 %shard_map.100 = bf16[64,2048]{1,0:T(8,128)(2,1)S(1)} custom-call(f32[64,2048]{1,0:T(8,128)} %refs_0_.1, f32[64,128]{1,0:T(8,128)} %refs_1_.1, f32[48,64]{1,0:T(8,128)} %refs_2_.1, f32[2,48,128]{2,1,0:T(8,128)} %refs_3_.1, f32[2,96,96]{2,1,0:T(8,128)} %refs_4_.1, f32[2,96,96]{2,1,0:T(8,128)} %refs_5_.1, f32[48,128]{1,0:T(8,128)} %refs_6_.1, ...), custom_call_target="tpu_custom_call" | custom-call | flops 491520000 | bytes 524288 | tf_op jit(solution)/shard_map/pallas_call | solution.py:387
  21.1 0.7 %copy.12 = bf16[64,2048]{1,0:T(8,128)(2,1)} copy(bf16[64,2048]{1,0:T(8,128)(2,1)S(1)} %shard_map.100) | data formatting | bytes 524288
